TPU v7x, 1024 devices: a whole 4x8x16 slice. The times are simulated.
1024 devices in a mesh: depth: 64 (over x_hi, z, core), chan: 16 (over y, x_lo).
Axes of the slice: x: 4 (x_hi: 2, x_lo: 2; x = x_hi * 2 + x_lo), y: 8, z: 16, core: 2. Of those that a mesh axis runs over, the one named last changes fastest.
Arguments:
- activations: bfloat16 [64, 64, 32, 128], P('chan', 'depth'), may hold values from -6 to 6
- slopes: bfloat16 [128, 64, 32, 128], P('chan', 'depth'), may hold values from -6 to 6
- weight: bfloat16 [27, 64, 128], replicated, may hold values from -0.15625 to 0.15625
Outputs:
- inputs_grad: bfloat16 [64, 64, 32, 128], P('chan', 'depth')
- weight_grad: float32 [27, 64, 128], P(None, None, 'chan')
All inputs are finite; a program needn't handle non-finite values.
Results may differ from a plain program's by a relative error of at most 0.0015.
Values may be sent and summed in bfloat16 or wider, within the bound.
A program may use at most 32 MiB of HBM per device.

v0:
```python
import math

import jax
import jax.numpy as jnp
from jax import lax
from jax.sharding import PartitionSpec as P


def padded(block, sides, width):
    for axis, dim in sides:
        count = lax.axis_size(axis)
        forward = [(i, i + 1) for i in range(count - 1)]
        backward = [(target, source) for source, target in forward]
        low = lax.ppermute(
            lax.slice_in_dim(block, block.shape[dim] - width, None, axis=dim), axis, forward
        )
        high = lax.ppermute(lax.slice_in_dim(block, 0, width, axis=dim), axis, backward)
        block = jnp.concatenate([low, block, high], axis=dim)
    return block


def input_term(slopes_halo, kernel_part, row_pad):
    return lax.conv_general_dilated(
        slopes_halo[None],
        kernel_part,
        (1, 1, 1),
        ((0, 0), (row_pad, row_pad), (1, 1)),
        dimension_numbers=("NCDHW", "DHWOI", "NCDHW"),
        preferred_element_type=jnp.float32,
    )[0]


def filter_grad(slopes_halo, inputs_part, row_pad):
    result = lax.conv_general_dilated(
        slopes_halo[:, None],
        inputs_part[:, None],
        (1, 1, 1),
        ((0, 0), (row_pad, row_pad), (1, 1)),
        dimension_numbers=("NCDHW", "OIDHW", "NCDHW"),
        preferred_element_type=jnp.float32,
    )
    result = result[:, :, ::-1, ::-1, ::-1]
    return jnp.transpose(result.reshape(result.shape[0], result.shape[1], 27), (2, 1, 0))


def per_device(activations, slopes, weight):
    cin_dev = activations.shape[0]
    planes, plane_rows, plane_cols = (
        activations.shape[1],
        activations.shape[2],
        activations.shape[3],
    )
    cell_count = planes * lax.axis_size("depth") * plane_rows * plane_cols
    scaling = 1.0 / math.sqrt(cell_count)
    kernel = weight.reshape(3, 3, 3, weight.shape[1], weight.shape[2])[::-1, ::-1, ::-1]
    padded_slopes = padded(slopes, (("depth", 1),), 1)
    chan_index = lax.axis_index("chan")
    all_slopes = lax.all_gather(padded_slopes, "chan", axis=0, tiled=True)
    kernel_part = lax.dynamic_slice_in_dim(kernel, chan_index * cin_dev, cin_dev, 3)
    inputs_grad = input_term(all_slopes, kernel_part, 1).astype(jnp.bfloat16)
    partial_value = filter_grad(all_slopes, activations, 1) * scaling
    summed = lax.psum(partial_value, "depth")
    weight_grad = lax.all_to_all(summed, "chan", split_axis=2, concat_axis=1, tiled=True)
    return (inputs_grad, weight_grad)


def solution(mesh):
    placed = (P("chan", "depth", None, None), P("chan", "depth", None, None), P())
    return jax.shard_map(
        per_device,
        mesh=mesh,
        in_specs=placed,
        out_specs=(P("chan", "depth", None, None), P(None, None, "chan")),
        check_vma=False,
    )
```

profile of v0, /device:TPU:2, one launch (start us, length us, event | category | flops | bytes accessed | tf_op | source)
XLA Modules:
  0.0 519.8 jit_solution(7830808502895252773)
XLA Ops:
  7.2 0.0 all-gather.2.cloned.1.call-start
  7.2 1.3 collective-permute-start.1
  8.5 3.0 collective-permute-start
  11.5 0.0 collective-permute-done.1
  11.6 1.1 collective-permute-done
  12.6 1.5 pad_maximum_fusion
  14.2 0.0 all-gather.2.cloned.1.call-update
  14.2 1.8 rev.6
  16.0 3.6 copy.40
  19.6 96.6 %all-gather.2.cloned.1.call-done = bf16[128,3,32,128]{3,2,1,0:T(8,128)(2,1)} async-done(((bf16[8,3,32,128]{3,2,1,0:T(8,128)(2,1)}), bf16[128,3,32,128]{3,2,1,0:T(8,128)(2,1)}) %all-gather.2.cloned.1.call-update) | async-done | bytes 3145744 | tf_op jit(solution)/shard_map/all_gather | solution.py:58
  116.3 4.6 copy.34
  120.9 0.6 pad
  121.4 1.3 copy.36
  122.7 0.1 slice.2
  122.9 0.0 copy-start.1
  122.9 0.0 copy-start
  122.9 69.9 %fusion.3 = bf16[1,32,8,17,4]{2,4,3,1,0:T(4,128)(2,1)} fusion(bf16[128,3,32,1,7,2]{0,4,5,2,1,3:T(8,128)(2,1)S(1)} %slice.2, bf16[128,3,32,1,8,17]{0,4,5,2,1,3:T(8,128)(2,1)S(1)} %copy.36, bf16[3,3,3,64,128]{4,3,2,1,0:T(8,128)(2,1)} %rev.6, s32[]{:T(128)S(6)} %select_n.3), kind=kOutput, calls=%fused_computation.4 | convolution fusion | flops 129024000 | bytes 3748868 | tf_op jit(solution)/shard_map/conv_general_dilated | solution.py:23
  192.8 1.3 copy.37
  194.1 0.1 select_convert_fusion
  194.2 0.1 copy.38
  194.3 7.1 %copy.39 = bf16[128,1,3,32,128]{0,1,4,3,2:T(2,128)(2,1)} copy(bf16[128,1,3,32,128]{4,3,2,0,1:T(8,128)(2,1)S(1)} %bitcast.27) | data formatting | bytes 6291456 | tf_op jit(solution)/shard_map/broadcast_in_dim | solution.py:35
  201.4 34.5 %fusion.11 = f32[128,4,3,3,3]{0,1,4,3,2:T(4,128)S(1)} fusion(bf16[128,1,3,32,128]{0,1,4,3,2:T(2,128)(2,1)} %copy.39, bf16[4,1,1,32,128]{0,1,4,3,2:T(2,128)(2,1)} %copy.40), kind=kOutput, calls=%fused_computation.16 | convolution fusion | flops 110309376 | bytes 3233792 | tf_op jit(solution)/shard_map/conv_general_dilated | solution.py:34
  236.0 0.2 copy.41
  236.1 256.7 %psum.7 = f32[27,4,128]{0,1,2:T(4,128)S(1)} all-reduce(f32[27,4,128]{0,1,2:T(4,128)S(1)} %bitcast.28), channel_id=1, replica_groups=mesh['depth'=64,'chan'=16] {'depth'}, use_global_device_ids=true, to_apply=%region_0.0 | all-reduce | flops 13824 | bytes 110592 | tf_op jit(solution)/shard_map/psum | solution.py:62
  492.8 1.0 reshape.36
  493.7 8.7 %all-to-all-start = ((f32[16,1,864]{2,1,0:T(1,128)}), f32[16,1,864]{2,1,0:T(1,128)S(1)}, u32[]{:S(2)}, u32[]{:S(2)}) async-start(f32[16,1,864]{2,1,0:T(1,128)} %reshape.36), calls=%async_computation | async-start | bytes 114688 | tf_op jit(solution)/shard_map/all_to_all | solution.py:63
  502.4 0.7 copy.44
  503.2 6.9 %all-to-all-done = f32[16,1,864]{2,1,0:T(1,128)S(1)} async-done(((f32[16,1,864]{2,1,0:T(1,128)}), f32[16,1,864]{2,1,0:T(1,128)S(1)}, u32[]{:S(2)}, u32[]{:S(2)}) %all-to-all-start) | async-done | bytes 55328 | tf_op jit(solution)/shard_map/all_to_all | solution.py:63
  510.1 0.5 broadcast.16
  510.6 0.8 reduce
  511.4 0.3 reshape.37
  511.8 0.8 copy.45
  (6 shorter events, 0.1 us)
Async XLA Ops:
  7.2 109.1 %all-gather.2.cloned.1.call-start = ((), (), s32[]{:S(2)}) async-start(), calls=%async_computation.1 | async-start | bytes 3342336 | tf_op jit(solution)/shard_map/all_gather | solution.py:58
  7.2 4.3 collective-permute-start.1
  8.5 4.1 collective-permute-start
  122.9 71.3 %copy-start.1 = (pred[8,17]{0,1:T(8,128)(4,1)S(1)}, pred[8,17]{0,1:T(8,128)(4,1)}, u32[]{:S(2)}) copy-start(pred[8,17]{0,1:T(8,128)(4,1)} %constant.18) | copy-start | bytes 412
  122.9 71.4 %copy-start = (bf16[128,3,32,128]{3,2,1,0:T(8,128)(2,1)S(1)}, bf16[128,3,32,128]{3,2,1,0:T(8,128)(2,1)}, u32[]{:S(2)}) copy-start(bf16[128,3,32,128]{3,2,1,0:T(8,128)(2,1)} %all-gather.2.cloned.1.call-done) | copy-start | bytes 9437188
  493.7 16.3 %all-to-all-start = ((f32[16,1,864]{2,1,0:T(1,128)}), f32[16,1,864]{2,1,0:T(1,128)S(1)}, u32[]{:S(2)}, u32[]{:S(2)}) async-start(f32[16,1,864]{2,1,0:T(1,128)} %reshape.36), calls=%async_computation | async-start | bytes 114688 | tf_op jit(solution)/shard_map/all_to_all | solution.py:63
Sparse Core Ops, SparseCore 0:
  14.3 101.8 all-gather.1
where the time goes:
time: 530 us; the launch traced here: 520 us
  blocking collectives  257 us (48%)
  waiting for transfers between devices  105 us (20%)
  matrix products  104 us (20%)
  local copies, waits for them, and re-layouts  24.1 us (5%)
  between operations  14.6 us (3%)
  starting transfers between devices  13 us (2%)
    psum x1, blocking collectives, per_device(): summed = lax.psum(partial_value, 'depth')  257 us
    all_gather x1, waiting for transfers between devices, per_device(): all_slopes = lax.all_gather(padded_slopes, 'chan', axis=0, tiled=True)  96.6 us
    conv_general_dilated x1, matrix products, input_term(): lax.conv_general_dilated(slopes_halo[None], kernel_part, (1, 1, 1), ((0,...  69.9 us
    conv_general_dilated x1, matrix products, filter_grad(): lax.conv_general_dilated(slopes_halo[:, None], inputs_part[:, None], (1,...  34.5 us
  transfers between devices with their start and end apart: 4, of which 3 were waited for; matrix products, arithmetic and copies ran while one was open for 1% of the time, Pallas kernels for 0%

commit v1 on v0

v1 whole, which is shorter than its diff:
```python
import math

import jax
import jax.numpy as jnp
from jax import lax
from jax.experimental import pallas as pl
from jax.experimental.pallas import tpu as pltpu
from jax.sharding import PartitionSpec as P

MESH = pl.DeviceIdType.MESH
F32, BF16 = jnp.float32, jnp.bfloat16
ND, NC = 64, 16
NZ = 16
PIECES = 56


def far_first():
    offsets = [(xh, dz, k) for xh in range(2) for dz in range(NZ) for k in range(2)]
    offsets.sort(key=lambda o: -(20 * o[0] + 10 * min(o[1], NZ - o[1]) + o[2]))
    return offsets[:-1]


DEPTH_OFFSETS = far_first()
CHAN_OFFSETS = (8, 9, 6, 10, 7, 11, 4, 12, 5, 13, 2, 14, 3, 15, 1)


def moved(d, offset):
    xh, dz, k = offset
    z = lax.rem(lax.rem(d // 2, NZ) + dz, NZ)
    return ((d // 32) ^ xh) * 32 + z * 2 + (lax.rem(d, 2) ^ k)


def owned(d):
    return d - d // 8


def owns(d):
    return lax.rem(d, 8) != 7


def drained(ref, sem):
    pltpu.make_async_copy(ref, ref, sem).wait()


def kernel(
    act_in, slopes_in, weight_in,
    grad_out, filt_out,
    act_all, slopes_all, weight_v, slopes_f, act_f, taps, act_taps,
    rows_send, rows_recv, rows_taps, near_send, near_recv, back_send, back_recv,
    piece_send, piece_recv, piece_sum, gathered, spread,
    local_sem, send_sem, recv_sem,
):
    d, c = lax.axis_index("depth"), lax.axis_index("chan")
    y, x = c // 2, lax.rem(c, 2)
    up, down = lax.rem(d + 1, ND), lax.rem(d + ND - 1, ND)
    other = c ^ 1

    loads = [
        pltpu.make_async_copy(slopes_in, slopes_all.at[2 + x], local_sem.at[0]),
        pltpu.make_async_copy(act_in, act_all.at[y], local_sem.at[1]),
        pltpu.make_async_copy(weight_in, weight_v, local_sem.at[2]),
    ]
    for load in loads:
        load.start()

    depth_peers = [(moved(d, o), c) for o in DEPTH_OFFSETS]
    chan_peers = [(d, lax.rem(c + k, NC)) for k in CHAN_OFFSETS]
    diagonal = [(up, other), (down, other)]
    greeted = depth_peers + chan_peers + diagonal
    barrier = pltpu.get_barrier_semaphore()
    for peer in greeted:
        pl.semaphore_signal(barrier, inc=1, device_id=peer, device_id_type=MESH)

    def send(src, dst, group, peer):
        pltpu.make_async_remote_copy(
            src_ref=src, dst_ref=dst, send_sem=send_sem.at[group],
            recv_sem=recv_sem.at[group], device_id=peer, device_id_type=MESH,
        ).start()

    lane = lax.broadcasted_iota(jnp.int32, (16, 128), 1)

    loads[0].wait()
    slopes_f[0:256] = slopes_all[2 + x].astype(F32)
    zero8 = jnp.zeros((8, 128), F32)

    def own_row(h):
        return slopes_f[pl.ds(h, 8, stride=32), :] if 0 <= h < 32 else zero8

    for p in range(NC):
        block = [own_row(2 * p - 1 + j) for j in range(4)]
        rows_send[p] = jnp.concatenate(block, axis=0).astype(BF16)
    rows_recv[c] = rows_send[c]
    act_taps[0:32, 128:256] = jnp.zeros((32, 128), BF16)
    act_taps[64:96, 4096:4224] = jnp.zeros((32, 128), BF16)
    act_taps[96:128, :] = jnp.zeros((32, 34 * 128), BF16)
    source = lax.broadcasted_iota(jnp.int32, (256, 256), 0)
    target = lax.broadcasted_iota(jnp.int32, (256, 256), 1)
    slot = (target & 3) * 8 + ((target & 63) >> 3) + ((target >> 6) * 32) + ((target >> 2) & 1) * 128
    spread[...] = jnp.where(source == slot, 1.0, 0.0).astype(BF16)

    loads[1].wait()
    pl.semaphore_wait(barrier, len(greeted))

    for k in (4, 3, 5, 2, 6, 1, 7):
        send(act_all.at[y], act_all.at[y], 0, (d, lax.rem(c + 2 * k, NC)))
    own = slopes_all.at[2 + x]
    send(own, slopes_all.at[4 + x], 1, (up, other))
    send(own, slopes_all.at[x], 1, (down, other))
    send(own, slopes_all.at[2 + x], 1, (d, other))
    send(own, slopes_all.at[4 + x], 1, (up, c))
    send(own, slopes_all.at[x], 1, (down, c))
    for peer in chan_peers:
        send(rows_send.at[peer[1]], rows_recv.at[c], 2, peer)

    drained(slopes_all.at[pl.ds(0, 5)], recv_sem.at[1])
    has_up = jnp.where(d == ND - 1, 0.0, 1.0).astype(F32)
    has_down = jnp.where(d == 0, 0.0, 1.0).astype(F32)
    for a in range(3):
        for xx in range(2):
            value = slopes_all[2 * a + xx].astype(F32)
            if a == 0:
                value = value * has_up
            if a == 2:
                value = value * has_down
            slopes_f[(2 * a + xx) * 256:(2 * a + xx + 1) * 256] = value

    def slope_rows(step, carry):
        for part in range(4):
            h = step * 4 + part
            at = pl.ds(pl.multiple_of(h * 128, 128), 128)
            for a in range(3):
                row = jnp.concatenate(
                    [slopes_f[pl.ds((2 * a + xx) * 256 + h, 8, stride=32), :] for xx in range(2)], axis=0
                )
                left = jnp.where(lane == 127, 0.0, pltpu.roll(row, 127, 1))
                right = jnp.where(lane == 0, 0.0, pltpu.roll(row, 1, 1))
                for third, value in enumerate((left, row, right)):
                    at_row = (3 * a + third) * 16
                    taps[at_row:at_row + 16, at] = value.astype(BF16)
        return carry

    lax.fori_loop(0, 8, slope_rows, 0)

    drained(act_all.at[pl.ds(0, 7)], recv_sem.at[0])
    for p in range(8):
        act_f[p * 128:(p + 1) * 128] = act_all[p].astype(F32)

    def act_rows(step, carry):
        for part in range(4):
            h = step * 4 + part
            row = jnp.concatenate(
                [act_f[pl.ds(i * 32 + h, 8, stride=128), :] for i in range(4)], axis=0
            ).astype(BF16)
            for b in range(3):
                at = pl.ds(pl.multiple_of((h + 2 - b) * 128, 128), 128)
                act_taps[b * 32:(b + 1) * 32, at] = row
        return carry

    lax.fori_loop(0, 8, act_rows, 0)
    terms = lax.dot_general(
        taps[...], act_taps[:, 128:4224], (((1,), (1,)), ((), ())), preferred_element_type=F32
    )

    lane8 = lax.broadcasted_iota(jnp.int32, (8, 128), 1)
    for xx in range(2):
        def tile(a, third):
            at_row = (3 * a + third) * 16 + xx * 8
            return terms[at_row:at_row + 8]
        packed = []
        for a in range(3):
            last = tile(a, 2)
            packed.append(jnp.where(lane8 < 96, tile(a, 0), pltpu.roll(last, 96, 1)))
            packed.append(jnp.where(lane8 < 96, tile(a, 1), pltpu.roll(last, 64, 1)))
        rest = jnp.zeros((8, 128), F32)
        for a in range(3):
            part = pltpu.roll(tile(a, 2), (32 * a - 64) % 128, 1)
            rest = jnp.where((lane8 >= 32 * a) & (lane8 < 32 * a + 32), part, rest)
        packed.append(rest)
        for t in range(7):
            for j in range(4):
                piece_send[xx * 28 + t * 4 + j] = packed[t][2 * j:2 * j + 2]

    for peer in depth_peers:
        @pl.when(owns(peer[0]))
        def _():
            send(piece_send.at[owned(peer[0])], piece_recv.at[d], 3, peer)

    @pl.when(owns(d))
    def _():
        piece_recv[d] = piece_send[owned(d)]

    loads[2].wait()
    drained(rows_recv.at[pl.ds(0, 15)], recv_sem.at[2])
    lane128 = lax.broadcasted_iota(jnp.int32, (128, 128), 1)
    for j in range(4):
        row = rows_recv[:, j * 8:(j + 1) * 8, :].astype(F32).reshape(128, 128)
        left = jnp.where(lane128 == 127, 0.0, pltpu.roll(row, 127, 1))
        right = jnp.where(lane128 == 0, 0.0, pltpu.roll(row, 1, 1))
        for third, value in enumerate((left, row, right)):
            rows_taps[third * 128:(third + 1) * 128, j * 128:(j + 1) * 128] = value.astype(BF16)
    right_side = jnp.concatenate(
        [rows_taps[:, (2 - b) * 128:(4 - b) * 128] for b in range(3)], axis=0
    )

    def plane_term(a):
        left_side = jnp.concatenate(
            [weight_v[(9 * a + k) * 64:(9 * a + k + 1) * 64] for k in range(9)], axis=1
        )
        return jnp.dot(left_side, right_side, preferred_element_type=F32)

    near_send[0] = plane_term(0)
    send(near_send.at[0], near_recv.at[0], 4, (down, c))
    near_send[1] = plane_term(2)
    send(near_send.at[1], near_recv.at[1], 4, (up, c))
    middle = plane_term(1)
    drained(near_recv, recv_sem.at[4])
    whole = middle + near_recv[0] * has_up + near_recv[1] * has_down
    for p in range(NC):
        back_send[p * 8:(p + 1) * 8] = jnp.concatenate(
            [whole[4 * p:4 * p + 4, 0:128], whole[4 * p:4 * p + 4, 128:256]], axis=0
        )
    mine = pl.ds(pl.multiple_of(c * 8, 8), 8)
    back_recv[mine] = back_send[mine]
    for peer in chan_peers:
        theirs = pl.ds(pl.multiple_of(peer[1] * 8, 8), 8)
        send(back_send.at[theirs], back_recv.at[mine], 5, peer)

    @pl.when(owns(d))
    def _():
        drained(piece_recv.at[pl.ds(0, 63)], recv_sem.at[3])
        piece_sum[...] = jnp.sum(piece_recv[...], axis=0)
        q = owned(d)
        to = q // 28
        slot_at = lax.rem(q, 28)
        goal = c - x + to
        for peer in depth_peers:
            send(piece_sum, gathered.at[x, slot_at], 6, (peer[0], goal))

        @pl.when(to == x)
        def _():
            gathered[x, slot_at] = piece_sum[...]

        @pl.when(to != x)
        def _():
            send(piece_sum, gathered.at[x, slot_at], 6, (d, goal))

    drained(back_recv.at[pl.ds(0, 120)], recv_sem.at[5])
    for i in range(4):
        grad_out[i] = back_recv[pl.ds(i, 32, stride=4), :].astype(BF16)

    kept = jnp.logical_and(owns(d), owned(d) // 28 == x)

    @pl.when(kept)
    def _():
        drained(piece_send.at[pl.ds(0, 55)], recv_sem.at[6])

    @pl.when(jnp.logical_not(kept))
    def _():
        drained(piece_send, recv_sem.at[6])

    sides = [gathered[xx].reshape(56, 128) for xx in range(2)]
    both = jnp.concatenate(sides, axis=1)
    high = both.astype(BF16)
    rest = both - high.astype(F32)
    mid = rest.astype(BF16)
    low = (rest - mid.astype(F32)).astype(BF16)
    split = jnp.concatenate([high.astype(F32), mid.astype(F32), low.astype(F32)], axis=0).astype(BF16)
    placed = jnp.dot(split, spread[...], preferred_element_type=F32)
    result = ((placed[0:56] + placed[56:112]) + placed[112:168]) * (1.0 / math.sqrt(ND * 32 * 128))
    for a in range(3):
        for b in range(3):
            for third in range(3):
                if third < 2:
                    t, part = 2 * a + third, b
                elif b < 2:
                    t, part = 2 * a + b, 3
                else:
                    t, part = 6, a
                filt_out[9 * a + 3 * b + third] = result[t * 8:t * 8 + 8, part * 64:part * 64 + 64]

    drained(act_all.at[pl.ds(0, 7)], send_sem.at[0])
    drained(slopes_all.at[pl.ds(0, 5)], send_sem.at[1])
    drained(rows_recv.at[pl.ds(0, 15)], send_sem.at[2])
    drained(near_send, send_sem.at[4])
    drained(back_send.at[pl.ds(0, 120)], send_sem.at[5])

    @pl.when(owns(d))
    def _():
        drained(piece_send.at[pl.ds(0, 55)], send_sem.at[3])

        @pl.when(owned(d) // 28 == x)
        def _():
            drained(piece_recv.at[pl.ds(0, 63)], send_sem.at[6])

        @pl.when(owned(d) // 28 != x)
        def _():
            drained(piece_recv, send_sem.at[6])

    @pl.when(jnp.logical_not(owns(d)))
    def _():
        drained(piece_send, send_sem.at[3])


def per_device(activations, slopes, weight):
    anywhere = pl.BlockSpec(memory_space=pl.ANY)
    vmem = pl.BlockSpec(memory_space=pltpu.VMEM)
    grad, filt = pl.pallas_call(
        kernel,
        name="conv_grads",
        out_shape=(
            jax.ShapeDtypeStruct((4, 32, 128), BF16),
            jax.ShapeDtypeStruct((27, 8, 64), F32),
        ),
        in_specs=[anywhere] * 3,
        out_specs=(vmem, vmem),
        scratch_shapes=[
            pltpu.VMEM((8, 128, 128), BF16),
            pltpu.VMEM((6, 256, 128), BF16),
            pltpu.VMEM((27 * 64, 128), BF16),
            pltpu.VMEM((6 * 256, 128), F32),
            pltpu.VMEM((8 * 128, 128), F32),
            pltpu.VMEM((144, 32 * 128), BF16),
            pltpu.VMEM((128, 34 * 128), BF16),
            pltpu.VMEM((NC, 32, 128), BF16),
            pltpu.VMEM((NC, 32, 128), BF16),
            pltpu.VMEM((384, 512), BF16),
            pltpu.VMEM((2, 64, 256), F32),
            pltpu.VMEM((2, 64, 256), F32),
            pltpu.VMEM((128, 128), F32),
            pltpu.VMEM((128, 128), F32),
            pltpu.VMEM((PIECES, 2, 128), F32),
            pltpu.VMEM((ND, 2, 128), F32),
            pltpu.VMEM((2, 128), F32),
            pltpu.VMEM((2, 28, 2, 128), F32),
            pltpu.VMEM((256, 256), BF16),
            pltpu.SemaphoreType.DMA((3,)),
            pltpu.SemaphoreType.DMA((7,)),
            pltpu.SemaphoreType.DMA((7,)),
        ],
        compiler_params=pltpu.CompilerParams(
            collective_id=0, has_side_effects=True, vmem_limit_bytes=32 * 1024 * 1024
        ),
    )(
        activations.reshape(128, 128),
        slopes.reshape(256, 128),
        weight.reshape(27 * 64, 128),
    )
    return grad.reshape(4, 1, 32, 128), jnp.transpose(filt, (0, 2, 1))


def solution(mesh):
    placed = (P("chan", "depth", None, None), P("chan", "depth", None, None), P())
    return jax.shard_map(
        per_device,
        mesh=mesh,
        in_specs=placed,
        out_specs=(P("chan", "depth", None, None), P(None, None, "chan")),
        check_vma=False,
    )
```

time: 530 us -> 55.4 us (0.10)
  the two profiles are of different devices: /device:TPU:2 before, /device:TPU:1 now
where the time goes in v1:
time: 55.4 us; the launch traced here: 55.1 us
  Pallas kernels  50.6 us (91%)
  local copies, waits for them, and re-layouts  3.86 us (7%)
  between operations  0.65 us (1%)
    pallas_call x1, Pallas kernels, per_device(): pl.pallas_call(kernel, name='conv_grads', out_shape=(jax.ShapeDtypeStruct...  50.6 us
    unnamed x8, local copies, waits for them, and re-layouts  3.86 us

profile of v1, /device:TPU:1, one launch (start us, length us, event | category | flops | bytes accessed | tf_op | source)
XLA Modules:
  0.0 55.1 jit_solution(2873039369144145305)
XLA Ops:
  0.6 0.0 copy-start
  0.6 1.0 %copy-done = bf16[27,64,128]{2,1,0:T(8,128)(2,1)S(1)} copy-done((bf16[27,64,128]{2,1,0:T(8,128)(2,1)S(1)}, bf16[27,64,128]{2,1,0:T(8,128)(2,1)}, u32[]{:S(2)}) %copy-start) | copy-done | bytes 442392
  1.6 0.0 copy-start.1
  1.6 0.8 %copy-done.1 = bf16[8,1,32,128]{3,2,1,0:T(8,128)(2,1)S(1)} copy-done((bf16[8,1,32,128]{3,2,1,0:T(8,128)(2,1)S(1)}, bf16[8,1,32,128]{3,2,1,0:T(8,128)(2,1)}, u32[]{:S(2)}) %copy-start.1) | copy-done | bytes 65560
  2.5 0.0 copy-start.2
  2.5 0.8 %copy-done.2 = bf16[4,1,32,128]{3,2,1,0:T(8,128)(2,1)S(1)} copy-done((bf16[4,1,32,128]{3,2,1,0:T(8,128)(2,1)S(1)}, bf16[4,1,32,128]{3,2,1,0:T(8,128)(2,1)}, u32[]{:S(2)}) %copy-start.2) | copy-done | bytes 32792
  3.2 50.6 %conv_grads.1 = (bf16[4,32,128]{2,1,0:T(8,128)(2,1)S(1)}, f32[27,8,64]{2,1,0:T(8,128)S(1)}) custom-call(bf16[128,128]{1,0:T(8,128)(2,1)S(1)} %bitcast.10, bf16[256,128]{1,0:T(8,128)(2,1)S(1)} %bitcast.9, bf16[1728,128]{1,0:T(8,128)(2,1)S(1)} %bitcast.7), custom_call_target="tpu_custom_call" | custom-call | tf_op jit(solution)/shard_map/conv_grads/pallas_call | solution.py:307
  53.8 0.6 %copy.8 = bf16[4,1,32,128]{3,2,1,0:T(8,128)(2,1)} copy(bf16[4,1,32,128]{3,2,1,0:T(8,128)(2,1)S(1)} %bitcast.11) | data formatting | bytes 65536
  54.4 0.6 %copy.9 = f32[27,64,8]{1,2,0:T(8,128)} copy(f32[27,64,8]{1,2,0:T(8,128)S(1)} %bitcast.8) | data formatting | bytes 110592
Async XLA Ops:
  0.6 1.0 %copy-start = (bf16[27,64,128]{2,1,0:T(8,128)(2,1)S(1)}, bf16[27,64,128]{2,1,0:T(8,128)(2,1)}, u32[]{:S(2)}) copy-start(bf16[27,64,128]{2,1,0:T(8,128)(2,1)} %param.5) | copy-start | bytes 1327108
  1.6 0.8 %copy-start.1 = (bf16[8,1,32,128]{3,2,1,0:T(8,128)(2,1)S(1)}, bf16[8,1,32,128]{3,2,1,0:T(8,128)(2,1)}, u32[]{:S(2)}) copy-start(bf16[8,1,32,128]{3,2,1,0:T(8,128)(2,1)} %param.4) | copy-start | bytes 196612
  2.5 0.8 %copy-start.2 = (bf16[4,1,32,128]{3,2,1,0:T(8,128)(2,1)S(1)}, bf16[4,1,32,128]{3,2,1,0:T(8,128)(2,1)}, u32[]{:S(2)}) copy-start(bf16[4,1,32,128]{3,2,1,0:T(8,128)(2,1)} %param.3) | copy-start | bytes 98308

commit v2 on v1

v2 whole, which is shorter than its diff:
```python
import math

import jax
import jax.numpy as jnp
from jax import lax
from jax.experimental import pallas as pl
from jax.experimental.pallas import tpu as pltpu
from jax.sharding import PartitionSpec as P

MESH = pl.DeviceIdType.MESH
F32, BF16 = jnp.float32, jnp.bfloat16
ND, NC = 64, 16
NZ = 16
NX = 2
LATE = 8
HAND_ON = ((1, ()), (2, ()), (3, ()), (4, (5, 6, 7, 8)), (15, (14, 13, 12, 11, 10, 9)))
CHAN_OFFSETS = (8, 9, 6, 10, 7, 11, 4, 12, 5, 13, 2, 14, 3, 15, 1)


def drained(ref, sem):
    pltpu.make_async_copy(ref, ref, sem).wait()


def kernel(
    act_in, slopes_in, weight_in,
    grad_out, filt_out,
    act_all, seam_act, terms, slopes_all, weight_v, slopes_f, act_f, taps, act_taps,
    rows_send, rows_recv, seam_send, seam_recv, rows_taps, near_send, near_recv, whole_sum, back_send, back_recv,
    quad_send, quad_recv, quarter, piece_recv, piece_sum, gathered, spread,
    local_sem, send_sem, recv_sem,
):
    d, c = lax.axis_index("depth"), lax.axis_index("chan")
    y, x = c // 2, lax.rem(c, 2)
    up, down = lax.rem(d + 1, ND), lax.rem(d + ND - 1, ND)
    other = c ^ 1

    loads = [
        pltpu.make_async_copy(slopes_in, slopes_all.at[2 + x], local_sem.at[0]),
        pltpu.make_async_copy(act_in, act_all.at[y], local_sem.at[1]),
        pltpu.make_async_copy(weight_in, weight_v, local_sem.at[2]),
    ]
    for load in loads:
        load.start()

    half_x, z, core = d // 32, lax.rem(d // 2, NZ), lax.rem(d, 2)
    chan_peers = [(d, lax.rem(c + k, NC)) for k in CHAN_OFFSETS]
    near = [(up, c), (down, c), (up, other), (down, other)]
    owner = z == 0
    barrier = pltpu.get_barrier_semaphore()

    def greet(peer):
        pl.semaphore_signal(barrier, inc=1, device_id=peer, device_id_type=MESH)

    def beside(k):
        return d, lax.rem(c + 2 * k + NC, NC)

    close = [beside(k) for k in (-2, 2, -1, 1)] + [(d, other), (d ^ 32, c), (d ^ 33, c), (down, c), (down, other)]
    seam = jnp.logical_and(owner, core == 0)
    tail = jnp.logical_and(z == NZ - 1, core == 1)
    for peer in close:
        greet(peer)

    @pl.when(jnp.logical_not(tail))
    def _():
        greet((up, c))
        greet((up, other))

    @pl.when(seam)
    def _():
        for k in range(1, 8):
            greet((down, lax.rem(c + 2 * k, NC)))

    @pl.when(owner)
    def _():
        for level in range(1, NZ):
            greet((half_x * 32 + level * 2 + core, c))

    def send(src, dst, group, peer):
        pltpu.make_async_remote_copy(
            src_ref=src, dst_ref=dst, send_sem=send_sem.at[group],
            recv_sem=recv_sem.at[group], device_id=peer, device_id_type=MESH,
        ).start()

    lane = lax.broadcasted_iota(jnp.int32, (16, 128), 1)

    loads[0].wait()
    loads[1].wait()

    @pl.when(seam)
    def _():
        pl.semaphore_wait(barrier, 9)

    @pl.when(jnp.logical_and(owner, core == 1))
    def _():
        pl.semaphore_wait(barrier, 11)

    @pl.when(tail)
    def _():
        pl.semaphore_wait(barrier, 19)

    @pl.when(jnp.logical_not(jnp.logical_or(owner, tail)))
    def _():
        pl.semaphore_wait(barrier, 12)

    def block(k):
        return lax.rem(y + k + 8, 8)

    for group, k in ((0, 2), (1, -2), (2, 1), (2, -1)):
        send(act_all.at[y], act_all.at[y], group, beside(k))
    own = slopes_all.at[2 + x]
    send(own, slopes_all.at[4 + x], 12, (up, other))
    send(own, slopes_all.at[2 + x], 3, (d, other))
    send(own, slopes_all.at[4 + x], 12, (up, c))

    @pl.when(jnp.logical_not(seam))
    def _():
        send(own, slopes_all.at[x], 3, (down, other))
        send(own, slopes_all.at[x], 3, (down, c))

    @pl.when(tail)
    def _():
        for k in (4, 3, 5, 2, 6, 1, 7, 0):
            send(act_all.at[y], seam_act.at[y], 16, (up, lax.rem(c + 2 * k, NC)))

    act_taps[0:32, 128:256] = jnp.zeros((32, 128), BF16)
    act_taps[64:96, 4096:4224] = jnp.zeros((32, 128), BF16)
    act_taps[96:128, :] = jnp.zeros((32, 34 * 128), BF16)
    source = lax.broadcasted_iota(jnp.int32, (256, 256), 0)
    target = lax.broadcasted_iota(jnp.int32, (256, 256), 1)
    slot = (target & 3) * 8 + ((target & 63) >> 3) + ((target >> 6) * 32) + ((target >> 2) & 1) * 128
    spread[...] = jnp.where(source == slot, 1.0, 0.0).astype(BF16)

    def convert(k):
        at = block(k)
        act_f[pl.ds(pl.multiple_of(at * 128, 128), 128)] = act_all[at].astype(F32)

    for group, k in ((0, 2), (1, -2)):
        drained(act_all.at[0], recv_sem.at[group])
        behind = block(-k)
        part = pl.ds(0 if k > 0 else 64, 64)
        send(act_all.at[behind, part], act_all.at[behind, part], 4, beside(k))
        send(act_all.at[behind], act_all.at[behind], 4, beside(k // 2))
    for k in (0, 2, -2):
        convert(k)

    @pl.when(tail)
    def _():
        drained(slopes_all.at[0], recv_sem.at[3])

    @pl.when(jnp.logical_not(tail))
    def _():
        drained(slopes_all.at[pl.ds(0, 3)], recv_sem.at[3])

    drained(slopes_all.at[pl.ds(0, 2)], recv_sem.at[12])
    has_up = jnp.where(d == ND - 1, 0.0, 1.0).astype(F32)
    has_down = jnp.where(d == 0, 0.0, 1.0).astype(F32)
    for a in range(3):
        for xx in range(2):
            value = slopes_all[2 * a + xx].astype(F32)
            if a == 0:
                value = jnp.where(tail, 0.0, value)
            if a == 2:
                value = value * has_down
            slopes_f[(2 * a + xx) * 256:(2 * a + xx + 1) * 256] = value

    def slope_rows(step, carry):
        for part in range(4):
            h = step * 4 + part
            at = pl.ds(pl.multiple_of(h * 128, 128), 128)
            for a in range(3):
                row = jnp.concatenate(
                    [slopes_f[pl.ds((2 * a + xx) * 256 + h, 8, stride=32), :] for xx in range(2)], axis=0
                )
                left = jnp.where(lane == 127, 0.0, pltpu.roll(row, 127, 1))
                right = jnp.where(lane == 0, 0.0, pltpu.roll(row, 1, 1))
                for third, value in enumerate((left, row, right)):
                    at_row = (3 * a + third) * 16
                    taps[at_row:at_row + 16, at] = value.astype(BF16)
        return carry

    lax.fori_loop(0, 8, slope_rows, 0)

    zero8 = jnp.zeros((8, 128), F32)

    def fill_rows(blocks, plane):
        def row(h):
            return slopes_f[pl.ds(plane * 256 + h, 8, stride=32), :] if 0 <= h < 32 else zero8

        for p in range(NC):
            block = [row(2 * p - 1 + j) for j in range(4)]
            blocks[p] = jnp.concatenate(block, axis=0).astype(BF16)

    fill_rows(rows_send, 2 + x)
    rows_recv[c] = rows_send[c]

    drained(act_all.at[pl.ds(0, 2)], recv_sem.at[2])
    convert(1)
    convert(-1)
    drained(act_all.at[pl.ds(0, 3)], recv_sem.at[4])
    for peer in chan_peers:
        send(rows_send.at[peer[1]], rows_recv.at[c], 5, peer)

    @pl.when(seam)
    def _():
        fill_rows(seam_send, 4 + x)
        seam_recv[c] = seam_send[c]
        for peer in chan_peers:
            send(seam_send.at[peer[1]], seam_recv.at[c], 15, peer)

    for k in (3, -3, 4):
        convert(k)

    def act_rows(step, carry):
        for part in range(4):
            h = step * 4 + part
            row = jnp.concatenate(
                [act_f[pl.ds(i * 32 + h, 8, stride=128), :] for i in range(4)], axis=0
            ).astype(BF16)
            for b in range(3):
                at = pl.ds(pl.multiple_of((h + 2 - b) * 128, 128), 128)
                act_taps[b * 32:(b + 1) * 32, at] = row
        return carry

    lax.fori_loop(0, 8, act_rows, 0)

    def filter_terms(rows):
        return lax.dot_general(
            rows, act_taps[:, 128:4224], (((1,), (1,)), ((), ())), preferred_element_type=F32
        )

    terms[...] = filter_terms(taps[...])

    @pl.when(seam)
    def _():
        drained(seam_act, recv_sem.at[16])
        for p in range(8):
            act_f[p * 128:(p + 1) * 128] = seam_act[p].astype(F32)
        lax.fori_loop(0, 8, act_rows, 0)
        terms[0:48] = terms[0:48] + filter_terms(taps[48:96]) * has_down

    lane8 = lax.broadcasted_iota(jnp.int32, (8, 128), 1)
    for xx in range(2):
        def tile(a, third):
            at_row = (3 * a + third) * 16 + xx * 8
            return terms[at_row:at_row + 8]
        packed = []
        for a in range(3):
            last = tile(a, 2)
            packed.append(jnp.where(lane8 < 96, tile(a, 0), pltpu.roll(last, 96, 1)))
            packed.append(jnp.where(lane8 < 96, tile(a, 1), pltpu.roll(last, 64, 1)))
        rest = jnp.zeros((8, 128), F32)
        for a in range(3):
            part = pltpu.roll(tile(a, 2), (32 * a - 64) % 128, 1)
            rest = jnp.where((lane8 >= 32 * a) & (lane8 < 32 * a + 32), part, rest)
        packed.append(rest)
        packed.append(jnp.zeros((8, 128), F32))
        for t in range(8):
            quad_send[t // 4, xx, t % 4] = packed[t]

    place = 2 * half_x + core
    for hop, k in ((1, 1), (1, 0), (0, 1)):
        to_x, to_core = half_x ^ hop, core ^ k
        send(quad_send.at[to_x, to_core], quad_recv.at[place], 6, (d ^ (32 * hop + k), c))
    quad_recv[place] = quad_send[half_x, core]

    @pl.when(jnp.logical_not(owner))
    def _():
        drained(quad_recv.at[pl.ds(0, 3)], recv_sem.at[6])
        quarter[...] = (quad_recv[0] + quad_recv[1]) + (quad_recv[2] + quad_recv[3])

    @pl.when(jnp.logical_and(z > 0, z < LATE))
    def _():
        send(quarter, piece_recv.at[z], 7, (half_x * 32 + core, c))

    @pl.when(z >= LATE)
    def _():
        send(quarter, piece_recv.at[z], 8, (half_x * 32 + core, c))

    loads[2].wait()
    drained(rows_recv.at[pl.ds(0, 15)], recv_sem.at[5])
    lane128 = lax.broadcasted_iota(jnp.int32, (128, 128), 1)

    def column_taps(blocks):
        for j in range(4):
            row = blocks[:, j * 8:(j + 1) * 8, :].astype(F32).reshape(128, 128)
            left = jnp.where(lane128 == 127, 0.0, pltpu.roll(row, 127, 1))
            right = jnp.where(lane128 == 0, 0.0, pltpu.roll(row, 1, 1))
            for third, value in enumerate((left, row, right)):
                rows_taps[third * 128:(third + 1) * 128, j * 128:(j + 1) * 128] = value.astype(BF16)

    def plane_term(a):
        left_side = jnp.concatenate(
            [weight_v[(9 * a + k) * 64:(9 * a + k + 1) * 64] for k in range(9)], axis=1
        )
        right_side = jnp.concatenate(
            [rows_taps[:, (2 - b) * 128:(4 - b) * 128] for b in range(3)], axis=0
        )
        return jnp.dot(left_side, right_side, preferred_element_type=F32)

    column_taps(rows_recv)
    near_send[0] = plane_term(0)
    send(near_send.at[0], near_recv.at[0], 9, (down, c))
    near_send[1] = plane_term(2)

    @pl.when(jnp.logical_not(tail))
    def _():
        send(near_send.at[1], near_recv.at[1], 14, (up, c))

    whole_sum[...] = plane_term(1)

    @pl.when(seam)
    def _():
        drained(seam_recv.at[pl.ds(0, 15)], recv_sem.at[15])
        column_taps(seam_recv)
        near_recv[1] = plane_term(2)

    @pl.when(jnp.logical_not(seam))
    def _():
        drained(near_recv.at[1], recv_sem.at[14])

    drained(near_recv.at[0], recv_sem.at[9])
    whole = whole_sum[...] + near_recv[0] * has_up + near_recv[1] * has_down
    for p in range(NC):
        back_send[p * 8:(p + 1) * 8] = jnp.concatenate(
            [whole[4 * p:4 * p + 4, 0:128], whole[4 * p:4 * p + 4, 128:256]], axis=0
        )
    mine = pl.ds(pl.multiple_of(c * 8, 8), 8)
    back_recv[mine] = back_send[mine]
    for peer in chan_peers:
        theirs = pl.ds(pl.multiple_of(peer[1] * 8, 8), 8)
        send(back_send.at[theirs], back_recv.at[mine], 10, peer)

    goal = c - x + core

    @pl.when(owner)
    def _():
        drained(quad_recv.at[pl.ds(0, 3)], recv_sem.at[6])
        total = (quad_recv[0] + quad_recv[1]) + (quad_recv[2] + quad_recv[3])
        drained(piece_recv.at[pl.ds(0, LATE - 1)], recv_sem.at[7])
        for k in range(1, LATE):
            total = total + piece_recv[k]
        drained(piece_recv.at[pl.ds(0, NZ - LATE)], recv_sem.at[8])
        for k in range(LATE, NZ):
            total = total + piece_recv[k]
        piece_sum[...] = total

        def give(peer):
            send(piece_sum, gathered.at[half_x, x], 11, peer)

        give((d ^ 33, goal))
        give((d ^ 32, goal))
        give((d ^ 1, goal))

        @pl.when(goal == c)
        def _():
            gathered[half_x, x] = total

        @pl.when(goal != c)
        def _():
            give((d, goal))

        for level, _ in HAND_ON:
            for hop in (1, 0):
                give(((half_x ^ hop) * 32 + level * 2 + half_x, goal))

    drained(back_recv.at[pl.ds(0, 120)], recv_sem.at[10])
    for i in range(4):
        grad_out[i] = back_recv[pl.ds(i, 32, stride=4), :].astype(BF16)

    kept = jnp.logical_and(owner, goal == c)

    @pl.when(kept)
    def _():
        drained(piece_recv.at[pl.ds(0, 3)], recv_sem.at[11])

    @pl.when(jnp.logical_and(owner, goal != c))
    def _():
        drained(piece_recv.at[pl.ds(0, 4)], recv_sem.at[11])

    @pl.when(jnp.logical_not(owner))
    def _():
        drained(piece_recv.at[pl.ds(0, 2)], recv_sem.at[11])
        send(gathered.at[core], gathered.at[core], 13, (d ^ 1, c))
        for level, followers in [pair for pair in HAND_ON if pair[1]]:
            @pl.when(z == level)
            def _():
                for follower in followers:
                    send(gathered.at[core], gathered.at[core], 11, (half_x * 32 + follower * 2 + core, c))

        drained(gathered.at[1 - core], recv_sem.at[13])

    sides = [
        jnp.concatenate([gathered[t // 4, xx, t % 4] for t in range(7)], axis=0) for xx in range(2)
    ]
    both = jnp.concatenate(sides, axis=1)
    high = both.astype(BF16)
    rest = both - high.astype(F32)
    mid = rest.astype(BF16)
    low = (rest - mid.astype(F32)).astype(BF16)
    split = jnp.concatenate([high.astype(F32), mid.astype(F32), low.astype(F32)], axis=0).astype(BF16)
    placed = jnp.dot(split, spread[...], preferred_element_type=F32)
    result = ((placed[0:56] + placed[56:112]) + placed[112:168]) * (1.0 / math.sqrt(ND * 32 * 128))
    for a in range(3):
        for b in range(3):
            for third in range(3):
                if third < 2:
                    t, part = 2 * a + third, b
                elif b < 2:
                    t, part = 2 * a + b, 3
                else:
                    t, part = 6, a
                filt_out[9 * a + 3 * b + third] = result[t * 8:t * 8 + 8, part * 64:part * 64 + 64]

    for group in (0, 1):
        drained(act_all.at[0], send_sem.at[group])
    drained(act_all.at[pl.ds(0, 2)], send_sem.at[2])
    drained(slopes_all.at[0], send_sem.at[3])
    drained(slopes_all.at[pl.ds(0, 2)], send_sem.at[12])
    drained(act_all.at[pl.ds(0, 3)], send_sem.at[4])
    drained(rows_recv.at[pl.ds(0, 15)], send_sem.at[5])
    drained(quad_recv.at[pl.ds(0, 3)], send_sem.at[6])
    drained(near_send.at[0], send_sem.at[9])
    drained(back_send.at[pl.ds(0, 120)], send_sem.at[10])

    @pl.when(seam)
    def _():
        drained(seam_recv.at[pl.ds(0, 15)], send_sem.at[15])

    @pl.when(jnp.logical_not(seam))
    def _():
        drained(slopes_all.at[pl.ds(0, 2)], send_sem.at[3])

    @pl.when(tail)
    def _():
        drained(seam_act, send_sem.at[16])

    @pl.when(jnp.logical_not(tail))
    def _():
        drained(near_send.at[1], send_sem.at[14])

    @pl.when(jnp.logical_and(z > 0, z < LATE))
    def _():
        drained(quarter, send_sem.at[7])

    @pl.when(z >= LATE)
    def _():
        drained(quarter, send_sem.at[8])

    @pl.when(owner)
    def _():
        drained(piece_recv.at[pl.ds(0, 3 + 2 * len(HAND_ON))], send_sem.at[11])

    @pl.when(jnp.logical_and(owner, goal != c))
    def _():
        drained(piece_recv.at[0], send_sem.at[11])

    @pl.when(jnp.logical_not(owner))
    def _():
        drained(gathered.at[0], send_sem.at[13])

    for level, followers in [pair for pair in HAND_ON if pair[1]]:
        @pl.when(z == level)
        def _():
            drained(piece_recv.at[pl.ds(0, 2 * len(followers))], send_sem.at[11])


def per_device(activations, slopes, weight):
    hbm = pl.BlockSpec(memory_space=pltpu.HBM)
    vmem = pl.BlockSpec(memory_space=pltpu.VMEM)
    grad, filt = pl.pallas_call(
        kernel,
        name="conv_grads",
        out_shape=(
            jax.ShapeDtypeStruct((4, 32, 128), BF16),
            jax.ShapeDtypeStruct((27, 8, 64), F32),
        ),
        in_specs=[hbm] * 3,
        out_specs=(vmem, vmem),
        scratch_shapes=[
            pltpu.VMEM((8, 128, 128), BF16),
            pltpu.VMEM((8, 128, 128), BF16),
            pltpu.VMEM((144, 128), F32),
            pltpu.VMEM((6, 256, 128), BF16),
            pltpu.VMEM((27 * 64, 128), BF16),
            pltpu.VMEM((6 * 256, 128), F32),
            pltpu.VMEM((8 * 128, 128), F32),
            pltpu.VMEM((144, 32 * 128), BF16),
            pltpu.VMEM((128, 34 * 128), BF16),
            pltpu.VMEM((NC, 32, 128), BF16),
            pltpu.VMEM((NC, 32, 128), BF16),
            pltpu.VMEM((NC, 32, 128), BF16),
            pltpu.VMEM((NC, 32, 128), BF16),
            pltpu.VMEM((384, 512), BF16),
            pltpu.VMEM((2, 64, 256), F32),
            pltpu.VMEM((2, 64, 256), F32),
            pltpu.VMEM((64, 256), F32),
            pltpu.VMEM((128, 128), F32),
            pltpu.VMEM((128, 128), F32),
            pltpu.VMEM((NX, 2, 4, 8, 128), F32),
            pltpu.VMEM((4, 4, 8, 128), F32),
            pltpu.VMEM((4, 8, 128), F32),
            pltpu.VMEM((NZ, 4, 8, 128), F32),
            pltpu.VMEM((4, 8, 128), F32),
            pltpu.VMEM((2, 2, 4, 8, 128), F32),
            pltpu.VMEM((256, 256), BF16),
            pltpu.SemaphoreType.DMA((3,)),
            pltpu.SemaphoreType.DMA((17,)),
            pltpu.SemaphoreType.DMA((17,)),
        ],
        compiler_params=pltpu.CompilerParams(
            collective_id=0, has_side_effects=True, vmem_limit_bytes=32 * 1024 * 1024
        ),
    )(
        pltpu.with_memory_space_constraint(activations.reshape(128, 128), pltpu.HBM),
        pltpu.with_memory_space_constraint(slopes.reshape(256, 128), pltpu.HBM),
        pltpu.with_memory_space_constraint(weight.reshape(27 * 64, 128), pltpu.HBM),
    )
    return grad.reshape(4, 1, 32, 128), jnp.transpose(filt, (0, 2, 1))


def solution(mesh):
    placed = (P("chan", "depth", None, None), P("chan", "depth", None, None), P())
    return jax.shard_map(
        per_device,
        mesh=mesh,
        in_specs=placed,
        out_specs=(P("chan", "depth", None, None), P(None, None, "chan")),
        check_vma=False,
    )
```

time: 55.4 us -> 46.6 us (0.84)
  Pallas kernels: 50.6 us -> 44.5 us
  local copies, waits for them, and re-layouts: 3.86 us -> 1.26 us
    pallas_call x1, Pallas kernels: 50.6 us -> 44.5 us  [per_device(): pl.pallas_call(kernel, name='conv_grads', out_shape=(jax.ShapeDtypeStruct...]
    unnamed x8 -> x2, local copies, waits for them, and re-layouts: 3.86 us -> 1.26 us
where the time goes in v2:
time: 46.6 us; the launch traced here: 46.4 us
  Pallas kernels  44.5 us (95%)
  local copies, waits for them, and re-layouts  1.26 us (3%)
  between operations  0.64 us (1%)
    pallas_call x1, Pallas kernels, per_device(): pl.pallas_call(kernel, name='conv_grads', out_shape=(jax.ShapeDtypeStruct...  44.5 us
    unnamed x2, local copies, waits for them, and re-layouts  1.26 us

profile of v2, /device:TPU:1, one launch (start us, length us, event | category | flops | bytes accessed | tf_op | source)
XLA Modules:
  0.0 46.4 jit_solution(11614101282067311017)
XLA Ops:
  0.6 44.5 %conv_grads.1 = (bf16[4,32,128]{2,1,0:T(8,128)(2,1)S(1)}, f32[27,8,64]{2,1,0:T(8,128)S(1)}) custom-call(bf16[128,128]{1,0:T(8,128)(2,1)} %bitcast.11, bf16[256,128]{1,0:T(8,128)(2,1)} %bitcast.10, bf16[1728,128]{1,0:T(8,128)(2,1)} %bitcast.9), custom_call_target="tpu_custom_call" | custom-call | tf_op jit(solution)/shard_map/conv_grads/pallas_call | solution.py:470
  45.2 0.6 %copy.8 = bf16[4,1,32,128]{3,2,1,0:T(8,128)(2,1)} copy(bf16[4,1,32,128]{3,2,1,0:T(8,128)(2,1)S(1)} %bitcast.8) | data formatting | bytes 65536
  45.8 0.6 %copy.9 = f32[27,64,8]{1,2,0:T(8,128)} copy(f32[27,64,8]{1,2,0:T(8,128)S(1)} %bitcast.7) | data formatting | bytes 110592

commit v3 on v2

--- a/solution.py
+++ b/solution.py
@@ -39,9 +39,6 @@
         pltpu.make_async_copy(act_in, act_all.at[y], local_sem.at[1]),
         pltpu.make_async_copy(weight_in, weight_v, local_sem.at[2]),
     ]
-    for load in loads:
-        load.start()
-
     half_x, z, core = d // 32, lax.rem(d // 2, NZ), lax.rem(d, 2)
     chan_peers = [(d, lax.rem(c + k, NC)) for k in CHAN_OFFSETS]
     near = [(up, c), (down, c), (up, other), (down, other)]
@@ -75,14 +72,15 @@
         for level in range(1, NZ):
             greet((half_x * 32 + level * 2 + core, c))
 
+    for load in loads:
+        load.start()
+
     def send(src, dst, group, peer):
         pltpu.make_async_remote_copy(
             src_ref=src, dst_ref=dst, send_sem=send_sem.at[group],
             recv_sem=recv_sem.at[group], device_id=peer, device_id_type=MESH,
         ).start()
 
-    lane = lax.broadcasted_iota(jnp.int32, (16, 128), 1)
-
     loads[0].wait()
     loads[1].wait()
 
@@ -108,13 +106,13 @@
     for group, k in ((0, 2), (1, -2), (2, 1), (2, -1)):
         send(act_all.at[y], act_all.at[y], group, beside(k))
     own = slopes_all.at[2 + x]
-    send(own, slopes_all.at[4 + x], 12, (up, other))
-    send(own, slopes_all.at[2 + x], 3, (d, other))
+    send(own, slopes_all.at[2 + x], 18, (d, other))
+    send(own, slopes_all.at[4 + x], 20, (up, other))
     send(own, slopes_all.at[4 + x], 12, (up, c))
 
     @pl.when(jnp.logical_not(seam))
     def _():
-        send(own, slopes_all.at[x], 3, (down, other))
+        send(own, slopes_all.at[x], 19, (down, other))
         send(own, slopes_all.at[x], 3, (down, c))
 
     @pl.when(tail)
@@ -124,7 +122,7 @@
 
     act_taps[0:32, 128:256] = jnp.zeros((32, 128), BF16)
     act_taps[64:96, 4096:4224] = jnp.zeros((32, 128), BF16)
-    act_taps[96:128, :] = jnp.zeros((32, 34 * 128), BF16)
+    terms[...] = jnp.zeros((160, 128), F32)
     source = lax.broadcasted_iota(jnp.int32, (256, 256), 0)
     target = lax.broadcasted_iota(jnp.int32, (256, 256), 1)
     slot = (target & 3) * 8 + ((target & 63) >> 3) + ((target >> 6) * 32) + ((target >> 2) & 1) * 128
@@ -143,44 +141,49 @@
     for k in (0, 2, -2):
         convert(k)
 
-    @pl.when(tail)
-    def _():
-        drained(slopes_all.at[0], recv_sem.at[3])
-
-    @pl.when(jnp.logical_not(tail))
-    def _():
-        drained(slopes_all.at[pl.ds(0, 3)], recv_sem.at[3])
-
-    drained(slopes_all.at[pl.ds(0, 2)], recv_sem.at[12])
     has_up = jnp.where(d == ND - 1, 0.0, 1.0).astype(F32)
     has_down = jnp.where(d == 0, 0.0, 1.0).astype(F32)
-    for a in range(3):
-        for xx in range(2):
+    zero8 = jnp.zeros((8, 128), F32)
+
+    def column_slopes(rel, up_group, down_group):
+        xx = x if rel == 0 else 1 - x
+
+        @pl.when(jnp.logical_not(tail))
+        def _():
+            drained(own, recv_sem.at[up_group])
+
+        drained(own, recv_sem.at[down_group])
+        if rel == 1:
+            drained(own, recv_sem.at[18])
+        for a in range(3):
             value = slopes_all[2 * a + xx].astype(F32)
             if a == 0:
                 value = jnp.where(tail, 0.0, value)
             if a == 2:
                 value = value * has_down
-            slopes_f[(2 * a + xx) * 256:(2 * a + xx + 1) * 256] = value
-
-    def slope_rows(step, carry):
-        for part in range(4):
-            h = step * 4 + part
-            at = pl.ds(pl.multiple_of(h * 128, 128), 128)
-            for a in range(3):
-                row = jnp.concatenate(
-                    [slopes_f[pl.ds((2 * a + xx) * 256 + h, 8, stride=32), :] for xx in range(2)], axis=0
-                )
-                left = jnp.where(lane == 127, 0.0, pltpu.roll(row, 127, 1))
-                right = jnp.where(lane == 0, 0.0, pltpu.roll(row, 1, 1))
-                for third, value in enumerate((left, row, right)):
-                    at_row = (3 * a + third) * 16
-                    taps[at_row:at_row + 16, at] = value.astype(BF16)
-        return carry
-
-    lax.fori_loop(0, 8, slope_rows, 0)
-
-    zero8 = jnp.zeros((8, 128), F32)
+            slopes_f[(2 * a + rel) * 256:(2 * a + rel + 1) * 256] = value
+
+        def slope_rows(step, carry):
+            for part in range(4):
+                h = step * 4 + part
+                at = pl.ds(pl.multiple_of(h * 128, 128), 128)
+                shifted = []
+                for a in range(3):
+                    row = slopes_f[pl.ds((2 * a + rel) * 256 + h, 8, stride=32), :]
+                    left = jnp.where(lane8 == 127, 0.0, pltpu.roll(row, 127, 1))
+                    right = jnp.where(lane8 == 0, 0.0, pltpu.roll(row, 1, 1))
+                    shifted += [left, row, right]
+                shifted.append(zero8)
+                for t in range(5):
+                    at_row = rel * 80 + t * 16
+                    both = jnp.concatenate(shifted[2 * t:2 * t + 2], axis=0)
+                    taps[at_row:at_row + 16, at] = both.astype(BF16)
+            return carry
+
+        lax.fori_loop(0, 8, slope_rows, 0)
+
+    lane8 = lax.broadcasted_iota(jnp.int32, (8, 128), 1)
+    column_slopes(0, 3, 12)
 
     def fill_rows(blocks, plane):
         def row(h):
@@ -190,8 +193,9 @@
             block = [row(2 * p - 1 + j) for j in range(4)]
             blocks[p] = jnp.concatenate(block, axis=0).astype(BF16)
 
-    fill_rows(rows_send, 2 + x)
+    fill_rows(rows_send, 2)
     rows_recv[c] = rows_send[c]
+    column_slopes(1, 19, 20)
 
     drained(act_all.at[pl.ds(0, 2)], recv_sem.at[2])
     convert(1)
@@ -202,7 +206,7 @@
 
     @pl.when(seam)
     def _():
-        fill_rows(seam_send, 4 + x)
+        fill_rows(seam_send, 4)
         seam_recv[c] = seam_send[c]
         for peer in chan_peers:
             send(seam_send.at[peer[1]], seam_recv.at[c], 15, peer)
@@ -225,24 +229,16 @@
 
     def filter_terms(rows):
         return lax.dot_general(
-            rows, act_taps[:, 128:4224], (((1,), (1,)), ((), ())), preferred_element_type=F32
+            rows, act_taps[0:96, 128:4224], (((1,), (1,)), ((), ())), preferred_element_type=F32
         )
 
-    terms[...] = filter_terms(taps[...])
-
-    @pl.when(seam)
-    def _():
-        drained(seam_act, recv_sem.at[16])
-        for p in range(8):
-            act_f[p * 128:(p + 1) * 128] = seam_act[p].astype(F32)
-        lax.fori_loop(0, 8, act_rows, 0)
-        terms[0:48] = terms[0:48] + filter_terms(taps[48:96]) * has_down
-
-    lane8 = lax.broadcasted_iota(jnp.int32, (8, 128), 1)
-    for xx in range(2):
+    place = 2 * half_x + core
+
+    def pack_and_send(rel):
         def tile(a, third):
-            at_row = (3 * a + third) * 16 + xx * 8
+            at_row = rel * 80 + (3 * a + third) * 8
             return terms[at_row:at_row + 8]
+
         packed = []
         for a in range(3):
             last = tile(a, 2)
@@ -253,14 +249,35 @@
             part = pltpu.roll(tile(a, 2), (32 * a - 64) % 128, 1)
             rest = jnp.where((lane8 >= 32 * a) & (lane8 < 32 * a + 32), part, rest)
         packed.append(rest)
-        packed.append(jnp.zeros((8, 128), F32))
-        for t in range(8):
-            quad_send[t // 4, xx, t % 4] = packed[t]
-
-    place = 2 * half_x + core
-    for hop, k in ((1, 1), (1, 0), (0, 1)):
-        to_x, to_core = half_x ^ hop, core ^ k
-        send(quad_send.at[to_x, to_core], quad_recv.at[place], 6, (d ^ (32 * hop + k), c))
+        to_core = 1 - x if rel == 0 else x
+        for h in range(NX):
+            quad_send[h, to_core, 0:24] = jnp.concatenate(packed[4 * h:4 * h + 3], axis=0)
+            quad_send[h, to_core, 24:28] = packed[3][4 * h:4 * h + 4]
+        here = d - core + to_core
+        send(quad_send.at[1 - half_x, to_core], quad_recv.at[place], 6, (here ^ 32, c))
+
+        @pl.when(to_core != core)
+        def _():
+            send(quad_send.at[half_x, to_core], quad_recv.at[place], 6, (d ^ 1, c))
+
+    terms[:, 0:96] = filter_terms(taps[...])
+    for rel in range(2):
+        @pl.when(jnp.logical_not(seam))
+        def _():
+            pack_and_send(rel)
+
+    @pl.when(seam)
+    def _():
+        drained(seam_act, recv_sem.at[16])
+        for p in range(8):
+            act_f[p * 128:(p + 1) * 128] = seam_act[p].astype(F32)
+        lax.fori_loop(0, 8, act_rows, 0)
+        for rel in range(2):
+            at_row = rel * 80
+            extra = filter_terms(taps[at_row + 16:at_row + 48])[8:32]
+            terms[at_row:at_row + 24, 0:96] = terms[at_row:at_row + 24, 0:96] + extra * has_down
+            pack_and_send(rel)
+
     quad_recv[place] = quad_send[half_x, core]
 
     @pl.when(jnp.logical_not(owner))
@@ -330,7 +347,7 @@
         theirs = pl.ds(pl.multiple_of(peer[1] * 8, 8), 8)
         send(back_send.at[theirs], back_recv.at[mine], 10, peer)
 
-    goal = c - x + core
+    goal = c - x + 1 - core
 
     @pl.when(owner)
     def _():
@@ -390,7 +407,10 @@
         drained(gathered.at[1 - core], recv_sem.at[13])
 
     sides = [
-        jnp.concatenate([gathered[t // 4, xx, t % 4] for t in range(7)], axis=0) for xx in range(2)
+        jnp.concatenate(
+            [gathered[0, xx, 0:24], gathered[0, xx, 24:28], gathered[1, xx, 24:28], gathered[1, xx, 0:24]], axis=0
+        )
+        for xx in range(2)
     ]
     both = jnp.concatenate(sides, axis=1)
     high = both.astype(BF16)
@@ -414,8 +434,8 @@
     for group in (0, 1):
         drained(act_all.at[0], send_sem.at[group])
     drained(act_all.at[pl.ds(0, 2)], send_sem.at[2])
-    drained(slopes_all.at[0], send_sem.at[3])
-    drained(slopes_all.at[pl.ds(0, 2)], send_sem.at[12])
+    for group in (12, 18, 20):
+        drained(own, send_sem.at[group])
     drained(act_all.at[pl.ds(0, 3)], send_sem.at[4])
     drained(rows_recv.at[pl.ds(0, 15)], send_sem.at[5])
     drained(quad_recv.at[pl.ds(0, 3)], send_sem.at[6])
@@ -428,7 +448,8 @@
 
     @pl.when(jnp.logical_not(seam))
     def _():
-        drained(slopes_all.at[pl.ds(0, 2)], send_sem.at[3])
+        drained(own, send_sem.at[3])
+        drained(own, send_sem.at[19])
 
     @pl.when(tail)
     def _():
@@ -462,6 +483,11 @@
         @pl.when(z == level)
         def _():
             drained(piece_recv.at[pl.ds(0, 2 * len(followers))], send_sem.at[11])
+
+
+def write_out(grad_in, filt_in, grad_out, filt_out):
+    grad_out[...] = grad_in[...]
+    filt_out[...] = filt_in[...]
 
 
 def per_device(activations, slopes, weight):
@@ -470,22 +496,19 @@
     grad, filt = pl.pallas_call(
         kernel,
         name="conv_grads",
-        out_shape=(
-            jax.ShapeDtypeStruct((4, 32, 128), BF16),
-            jax.ShapeDtypeStruct((27, 8, 64), F32),
-        ),
+        out_shape=(pltpu.VMEM((4, 32, 128), BF16), pltpu.VMEM((27, 8, 64), F32)),
         in_specs=[hbm] * 3,
         out_specs=(vmem, vmem),
         scratch_shapes=[
             pltpu.VMEM((8, 128, 128), BF16),
             pltpu.VMEM((8, 128, 128), BF16),
-            pltpu.VMEM((144, 128), F32),
+            pltpu.VMEM((160, 128), F32),
             pltpu.VMEM((6, 256, 128), BF16),
             pltpu.VMEM((27 * 64, 128), BF16),
             pltpu.VMEM((6 * 256, 128), F32),
             pltpu.VMEM((8 * 128, 128), F32),
-            pltpu.VMEM((144, 32 * 128), BF16),
-            pltpu.VMEM((128, 34 * 128), BF16),
+            pltpu.VMEM((160, 32 * 128), BF16),
+            pltpu.VMEM((96, 34 * 128), BF16),
             pltpu.VMEM((NC, 32, 128), BF16),
             pltpu.VMEM((NC, 32, 128), BF16),
             pltpu.VMEM((NC, 32, 128), BF16),
@@ -496,16 +519,16 @@
             pltpu.VMEM((64, 256), F32),
             pltpu.VMEM((128, 128), F32),
             pltpu.VMEM((128, 128), F32),
-            pltpu.VMEM((NX, 2, 4, 8, 128), F32),
-            pltpu.VMEM((4, 4, 8, 128), F32),
-            pltpu.VMEM((4, 8, 128), F32),
-            pltpu.VMEM((NZ, 4, 8, 128), F32),
-            pltpu.VMEM((4, 8, 128), F32),
-            pltpu.VMEM((2, 2, 4, 8, 128), F32),
+            pltpu.VMEM((NX, 2, 28, 128), F32),
+            pltpu.VMEM((4, 28, 128), F32),
+            pltpu.VMEM((28, 128), F32),
+            pltpu.VMEM((NZ, 28, 128), F32),
+            pltpu.VMEM((28, 128), F32),
+            pltpu.VMEM((2, 2, 28, 128), F32),
             pltpu.VMEM((256, 256), BF16),
             pltpu.SemaphoreType.DMA((3,)),
-            pltpu.SemaphoreType.DMA((17,)),
-            pltpu.SemaphoreType.DMA((17,)),
+            pltpu.SemaphoreType.DMA((21,)),
+            pltpu.SemaphoreType.DMA((21,)),
         ],
         compiler_params=pltpu.CompilerParams(
             collective_id=0, has_side_effects=True, vmem_limit_bytes=32 * 1024 * 1024
@@ -515,6 +538,16 @@
         pltpu.with_memory_space_constraint(slopes.reshape(256, 128), pltpu.HBM),
         pltpu.with_memory_space_constraint(weight.reshape(27 * 64, 128), pltpu.HBM),
     )
+    grad, filt = pl.pallas_call(
+        write_out,
+        name="write_out",
+        out_shape=(
+            jax.ShapeDtypeStruct((4, 32, 128), BF16),
+            jax.ShapeDtypeStruct((27, 8, 64), F32),
+        ),
+        in_specs=[vmem] * 2,
+        out_specs=(vmem, vmem),
+    )(pltpu.with_memory_space_constraint(grad, pltpu.VMEM), pltpu.with_memory_space_constraint(filt, pltpu.VMEM))
     return grad.reshape(4, 1, 32, 128), jnp.transpose(filt, (0, 2, 1))
 
 

time: 46.6 us -> 44.9 us (0.964)
  local copies, waits for them, and re-layouts: 1.26 us -> 0 us
    unnamed x2 -> x0, local copies, waits for them, and re-layouts: 1.26 us -> none
    pallas_call x1 -> x2, Pallas kernels: 44.5 us -> 44.1 us  [the longest x1 43.5 us: per_device(): pl.pallas_call(kernel, name='conv_grads', out_shape=(pltpu.VMEM((4, 32, 1...]
where the time goes in v3:
time: 44.9 us; the launch traced here: 44.8 us
  Pallas kernels  44.1 us (98%)
  between operations  0.64 us (1%)
    pallas_call x1, Pallas kernels, per_device(): pl.pallas_call(kernel, name='conv_grads', out_shape=(pltpu.VMEM((4, 32, 1...  43.5 us

profile of v3, /device:TPU:1, one launch (start us, length us, event | category | flops | bytes accessed | tf_op | source)
XLA Modules:
  0.0 44.8 jit_solution(6753885763345619944)
XLA Ops:
  0.6 43.5 %conv_grads.1 = (bf16[4,32,128]{2,1,0:T(8,128)(2,1)S(1)}, f32[27,8,64]{2,1,0:T(8,128)S(1)}) custom-call(bf16[128,128]{1,0:T(8,128)(2,1)} %bitcast.9, bf16[256,128]{1,0:T(8,128)(2,1)} %bitcast.8, bf16[1728,128]{1,0:T(8,128)(2,1)} %bitcast.7), custom_call_target="tpu_custom_call" | custom-call | tf_op jit(solution)/shard_map/conv_grads/pallas_call | solution.py:496
  44.1 0.7 %write_out.1 = (bf16[4,32,128]{2,1,0:T(8,128)(2,1)}, f32[27,8,64]{2,1,0:T(8,128)}) custom-call(bf16[4,32,128]{2,1,0:T(8,128)(2,1)S(1)} %get-tuple-element.6.grad_in, f32[27,8,64]{2,1,0:T(8,128)S(1)} %get-tuple-element.7.filt_in), custom_call_target="tpu_custom_call" | custom-call | tf_op jit(solution)/shard_map/write_out/pallas_call | solution.py:541

commit v4 on v3

--- a/solution.py
+++ b/solution.py
@@ -103,16 +103,22 @@
     def block(k):
         return lax.rem(y + k + 8, 8)
 
-    for group, k in ((0, 2), (1, -2), (2, 1), (2, -1)):
+    for group, k in ((0, 2), (1, -2)):
         send(act_all.at[y], act_all.at[y], group, beside(k))
     own = slopes_all.at[2 + x]
     send(own, slopes_all.at[2 + x], 18, (d, other))
-    send(own, slopes_all.at[4 + x], 20, (up, other))
     send(own, slopes_all.at[4 + x], 12, (up, c))
 
+    @pl.when(core == 1)
+    def _():
+        send(own, slopes_all.at[4 + x], 20, (up, other))
+
+    @pl.when(jnp.logical_and(core == 0, jnp.logical_not(seam)))
+    def _():
+        send(own, slopes_all.at[x], 19, (down, other))
+
     @pl.when(jnp.logical_not(seam))
     def _():
-        send(own, slopes_all.at[x], 19, (down, other))
         send(own, slopes_all.at[x], 3, (down, c))
 
     @pl.when(tail)
@@ -132,12 +138,26 @@
         at = block(k)
         act_f[pl.ds(pl.multiple_of(at * 128, 128), 128)] = act_all[at].astype(F32)
 
-    for group, k in ((0, 2), (1, -2)):
+    for group, k in ((1, -2), (0, 2)):
         drained(act_all.at[0], recv_sem.at[group])
         behind = block(-k)
         part = pl.ds(0 if k > 0 else 64, 64)
         send(act_all.at[behind, part], act_all.at[behind, part], 4, beside(k))
         send(act_all.at[behind], act_all.at[behind], 4, beside(k // 2))
+    for k in (1, -1):
+        send(act_all.at[y], act_all.at[y], 2, beside(k))
+
+    drained(own, recv_sem.at[18])
+    across = slopes_all.at[3 - x]
+
+    @pl.when(core == 0)
+    def _():
+        send(across, slopes_all.at[5 - x], 20, (up, c))
+
+    @pl.when(core == 1)
+    def _():
+        send(across, slopes_all.at[1 - x], 19, (down, c))
+
     for k in (0, 2, -2):
         convert(k)
 
@@ -153,8 +173,6 @@
             drained(own, recv_sem.at[up_group])
 
         drained(own, recv_sem.at[down_group])
-        if rel == 1:
-            drained(own, recv_sem.at[18])
         for a in range(3):
             value = slopes_all[2 * a + xx].astype(F32)
             if a == 0:
@@ -201,11 +219,14 @@
     convert(1)
     convert(-1)
     drained(act_all.at[pl.ds(0, 3)], recv_sem.at[4])
-    for peer in chan_peers:
-        send(rows_send.at[peer[1]], rows_recv.at[c], 5, peer)
+
+    def send_rows():
+        for peer in chan_peers:
+            send(rows_send.at[peer[1]], rows_recv.at[c], 5, peer)
 
     @pl.when(seam)
     def _():
+        send_rows()
         fill_rows(seam_send, 4)
         seam_recv[c] = seam_send[c]
         for peer in chan_peers:
@@ -234,10 +255,11 @@
 
     place = 2 * half_x + core
 
-    def pack_and_send(rel):
+    def pack_and_send(to_core):
+        rel = x if to_core == 1 else 1 - x
+
         def tile(a, third):
-            at_row = rel * 80 + (3 * a + third) * 8
-            return terms[at_row:at_row + 8]
+            return terms[pl.ds(pl.multiple_of(rel * 80 + (3 * a + third) * 8, 8), 8)]
 
         packed = []
         for a in range(3):
@@ -249,7 +271,6 @@
             part = pltpu.roll(tile(a, 2), (32 * a - 64) % 128, 1)
             rest = jnp.where((lane8 >= 32 * a) & (lane8 < 32 * a + 32), part, rest)
         packed.append(rest)
-        to_core = 1 - x if rel == 0 else x
         for h in range(NX):
             quad_send[h, to_core, 0:24] = jnp.concatenate(packed[4 * h:4 * h + 3], axis=0)
             quad_send[h, to_core, 24:28] = packed[3][4 * h:4 * h + 4]
@@ -261,22 +282,26 @@
             send(quad_send.at[half_x, to_core], quad_recv.at[place], 6, (d ^ 1, c))
 
     terms[:, 0:96] = filter_terms(taps[...])
-    for rel in range(2):
-        @pl.when(jnp.logical_not(seam))
-        def _():
-            pack_and_send(rel)
-
-    @pl.when(seam)
+
+    @pl.when(d != ND // 2)
+    def _():
+        for to_core in (1, 0):
+            pack_and_send(to_core)
+
+    pl.when(jnp.logical_not(seam))(send_rows)
+
+    @pl.when(d == ND // 2)
     def _():
         drained(seam_act, recv_sem.at[16])
         for p in range(8):
             act_f[p * 128:(p + 1) * 128] = seam_act[p].astype(F32)
         lax.fori_loop(0, 8, act_rows, 0)
+        extra = filter_terms(taps[16:128])
         for rel in range(2):
             at_row = rel * 80
-            extra = filter_terms(taps[at_row + 16:at_row + 48])[8:32]
-            terms[at_row:at_row + 24, 0:96] = terms[at_row:at_row + 24, 0:96] + extra * has_down
-            pack_and_send(rel)
+            terms[at_row:at_row + 24, 0:96] = terms[at_row:at_row + 24, 0:96] + extra[at_row + 8:at_row + 32]
+        for to_core in (1, 0):
+            pack_and_send(to_core)
 
     quad_recv[place] = quad_send[half_x, core]
 
@@ -364,8 +389,8 @@
         def give(peer):
             send(piece_sum, gathered.at[half_x, x], 11, peer)
 
+        give((d ^ 32, goal))
         give((d ^ 33, goal))
-        give((d ^ 32, goal))
         give((d ^ 1, goal))
 
         @pl.when(goal == c)
@@ -430,6 +455,10 @@
                 else:
                     t, part = 6, a
                 filt_out[9 * a + 3 * b + third] = result[t * 8:t * 8 + 8, part * 64:part * 64 + 64]
+
+    @pl.when(d == 0)
+    def _():
+        drained(seam_act, recv_sem.at[16])
 
     for group in (0, 1):
         drained(act_all.at[0], send_sem.at[group])

time: 44.9 us -> 44 us (0.980)
  Pallas kernels: 44.1 us -> 42.9 us
    pallas_call x1, Pallas kernels: 43.5 us -> 42.2 us  [per_device(): pl.pallas_call(kernel, name='conv_grads', out_shape=(pltpu.VMEM((4, 32, 1...]
where the time goes in v4:
time: 44 us; the launch traced here: 43.5 us
  Pallas kernels  42.9 us (98%)
  between operations  0.64 us (1%)
    pallas_call x1, Pallas kernels, per_device(): pl.pallas_call(kernel, name='conv_grads', out_shape=(pltpu.VMEM((4, 32, 1...  42.2 us

profile of v4, /device:TPU:1, one launch (start us, length us, event | category | flops | bytes accessed | tf_op | source)
XLA Modules:
  0.0 43.5 jit_solution(4701450852273487374)
XLA Ops:
  0.6 42.2 %conv_grads.1 = (bf16[4,32,128]{2,1,0:T(8,128)(2,1)S(1)}, f32[27,8,64]{2,1,0:T(8,128)S(1)}) custom-call(bf16[128,128]{1,0:T(8,128)(2,1)} %bitcast.9, bf16[256,128]{1,0:T(8,128)(2,1)} %bitcast.8, bf16[1728,128]{1,0:T(8,128)(2,1)} %bitcast.7), custom_call_target="tpu_custom_call" | custom-call | tf_op jit(solution)/shard_map/conv_grads/pallas_call | solution.py:525
  42.9 0.7 %write_out.1 = (bf16[4,32,128]{2,1,0:T(8,128)(2,1)}, f32[27,8,64]{2,1,0:T(8,128)}) custom-call(bf16[4,32,128]{2,1,0:T(8,128)(2,1)S(1)} %get-tuple-element.6.grad_in, f32[27,8,64]{2,1,0:T(8,128)S(1)} %get-tuple-element.7.filt_in), custom_call_target="tpu_custom_call" | custom-call | tf_op jit(solution)/shard_map/write_out/pallas_call | solution.py:570

commit v5 on v4

--- a/solution.py
+++ b/solution.py
@@ -13,7 +13,7 @@
 NZ = 16
 NX = 2
 LATE = 8
-HAND_ON = ((1, ()), (2, ()), (3, ()), (4, (5, 6, 7, 8)), (15, (14, 13, 12, 11, 10, 9)))
+HAND_ON = ((1, ()), (2, ()), (3, ()), (4, ()), (5, (6, 7, 8)), (15, (14, 13, 12, 11, 10, 9)))
 CHAN_OFFSETS = (8, 9, 6, 10, 7, 11, 4, 12, 5, 13, 2, 14, 3, 15, 1)
 
 
@@ -138,12 +138,25 @@
         at = block(k)
         act_f[pl.ds(pl.multiple_of(at * 128, 128), 128)] = act_all[at].astype(F32)
 
-    for group, k in ((1, -2), (0, 2)):
+    def hand_on(group, k):
         drained(act_all.at[0], recv_sem.at[group])
         behind = block(-k)
         part = pl.ds(0 if k > 0 else 64, 64)
         send(act_all.at[behind, part], act_all.at[behind, part], 4, beside(k))
         send(act_all.at[behind], act_all.at[behind], 4, beside(k // 2))
+
+    from_below = jnp.logical_and(y >= 2, y < 6)
+
+    @pl.when(from_below)
+    def _():
+        hand_on(0, 2)
+        hand_on(1, -2)
+
+    @pl.when(jnp.logical_not(from_below))
+    def _():
+        hand_on(1, -2)
+        hand_on(0, 2)
+
     for k in (1, -1):
         send(act_all.at[y], act_all.at[y], 2, beside(k))
 
@@ -534,8 +547,8 @@
             pltpu.VMEM((160, 128), F32),
             pltpu.VMEM((6, 256, 128), BF16),
             pltpu.VMEM((27 * 64, 128), BF16),
-            pltpu.VMEM((6 * 256, 128), F32),
-            pltpu.VMEM((8 * 128, 128), F32),
+            pltpu.VMEM((6 * 256 + 32, 128), F32),
+            pltpu.VMEM((9 * 128, 128), F32),
             pltpu.VMEM((160, 32 * 128), BF16),
             pltpu.VMEM((96, 34 * 128), BF16),
             pltpu.VMEM((NC, 32, 128), BF16),
@@ -547,7 +560,7 @@
             pltpu.VMEM((2, 64, 256), F32),
             pltpu.VMEM((64, 256), F32),
             pltpu.VMEM((128, 128), F32),
-            pltpu.VMEM((128, 128), F32),
+            pltpu.VMEM((136, 128), F32),
             pltpu.VMEM((NX, 2, 28, 128), F32),
             pltpu.VMEM((4, 28, 128), F32),
             pltpu.VMEM((28, 128), F32),

time: 44 us -> 44.1 us (level)
  no operation moved by 1% of the time
where the time goes in v5:
time: 44.1 us; the launch traced here: 43.9 us
  Pallas kernels  43.3 us (98%)
  between operations  0.64 us (1%)
    pallas_call x1, Pallas kernels, per_device(): pl.pallas_call(kernel, name='conv_grads', out_shape=(pltpu.VMEM((4, 32, 1...  42.6 us

profile of v5, /device:TPU:1, one launch (start us, length us, event | category | flops | bytes accessed | tf_op | source)
XLA Modules:
  0.0 43.9 jit_solution(12403120768748611250)
XLA Ops:
  0.6 42.6 %conv_grads.1 = (bf16[4,32,128]{2,1,0:T(8,128)(2,1)S(1)}, f32[27,8,64]{2,1,0:T(8,128)S(1)}) custom-call(bf16[128,128]{1,0:T(8,128)(2,1)} %bitcast.9, bf16[256,128]{1,0:T(8,128)(2,1)} %bitcast.8, bf16[1728,128]{1,0:T(8,128)(2,1)} %bitcast.7), custom_call_target="tpu_custom_call" | custom-call | tf_op jit(solution)/shard_map/conv_grads/pallas_call | solution.py:538
  43.3 0.7 %write_out.1 = (bf16[4,32,128]{2,1,0:T(8,128)(2,1)}, f32[27,8,64]{2,1,0:T(8,128)}) custom-call(bf16[4,32,128]{2,1,0:T(8,128)(2,1)S(1)} %get-tuple-element.6.grad_in, f32[27,8,64]{2,1,0:T(8,128)S(1)} %get-tuple-element.7.filt_in), custom_call_target="tpu_custom_call" | custom-call | tf_op jit(solution)/shard_map/write_out/pallas_call | solution.py:583

commit v6 on v5

--- a/solution.py
+++ b/solution.py
@@ -12,7 +12,7 @@
 ND, NC = 64, 16
 NZ = 16
 NX = 2
-LATE = 8
+LATE = 12
 HAND_ON = ((1, ()), (2, ()), (3, ()), (4, ()), (5, (6, 7, 8)), (15, (14, 13, 12, 11, 10, 9)))
 CHAN_OFFSETS = (8, 9, 6, 10, 7, 11, 4, 12, 5, 13, 2, 14, 3, 15, 1)
 

time: 44.1 us -> 44.1 us (level)
  no operation moved by 1% of the time
where the time goes in v6:
time: 44.1 us; the launch traced here: 44 us
  Pallas kernels  43.3 us (98%)
  between operations  0.64 us (1%)
    pallas_call x1, Pallas kernels, per_device(): pl.pallas_call(kernel, name='conv_grads', out_shape=(pltpu.VMEM((4, 32, 1...  42.6 us

profile of v6, /device:TPU:1, one launch (start us, length us, event | category | flops | bytes accessed | tf_op | source)
XLA Modules:
  0.0 44.0 jit_solution(16900246850603467701)
XLA Ops:
  0.6 42.6 %conv_grads.1 = (bf16[4,32,128]{2,1,0:T(8,128)(2,1)S(1)}, f32[27,8,64]{2,1,0:T(8,128)S(1)}) custom-call(bf16[128,128]{1,0:T(8,128)(2,1)} %bitcast.9, bf16[256,128]{1,0:T(8,128)(2,1)} %bitcast.8, bf16[1728,128]{1,0:T(8,128)(2,1)} %bitcast.7), custom_call_target="tpu_custom_call" | custom-call | tf_op jit(solution)/shard_map/conv_grads/pallas_call | solution.py:538
  43.3 0.7 %write_out.1 = (bf16[4,32,128]{2,1,0:T(8,128)(2,1)}, f32[27,8,64]{2,1,0:T(8,128)}) custom-call(bf16[4,32,128]{2,1,0:T(8,128)(2,1)S(1)} %get-tuple-element.6.grad_in, f32[27,8,64]{2,1,0:T(8,128)S(1)} %get-tuple-element.7.filt_in), custom_call_target="tpu_custom_call" | custom-call | tf_op jit(solution)/shard_map/write_out/pallas_call | solution.py:583
